TPU v7x, 32 devices: a whole 2x2x4 slice. The times are simulated.
32 devices in a mesh: grp: 2 (over y), ex: 4 (over z), blk: 2 (over x), rep: 2 (over core).
Axes of the slice: x: 2, y: 2, z: 4, core: 2. Of those that a mesh axis runs over, the one named last changes fastest.
Arguments:
- acts: bfloat16 [256, 64, 4096], P(('grp', 'ex'), None, 'blk'), parts along dimension 0, may hold values from -6 to 6
- grads: bfloat16 [256, 64, 4096], P(('grp', 'ex'), None, 'blk'), parts along dimension 0, may hold values from -6 to 6
- lengths: int32 [256], P(('grp', 'ex')), parts along dimension 0, may hold values from 16 to 64
- adapter_down_weight: bfloat16 [4096, 128], P('blk'), may hold values from -0.09375 to 0.09375
- adapter_up_weight: bfloat16 [128, 4096], P(None, 'blk'), may hold values from -0.09375 to 0.09375
- down_random_signs: int32 [4096, 512], P('blk'), may hold values from -1 to 1, as said below
- up_random_signs: int32 [4096, 512], P('blk'), may hold values from -1 to 1, as said below
- mixer: int32 [256, 16], P(None, 'rep'), may hold values from -1 to 1, as said below
- validation_feature_rows: bfloat16 [512, 512, 16], P('ex', 'blk', 'rep'), may hold values from -6 to 6
- validation_task_index: int32 [512], replicated, may hold values from 0 to 7, never falling along the last dimension, each value on 1 to 128 neighbouring positions
Outputs:
- similarity: float32 [256, 512], P(('grp', 'ex')), parts along dimension 0
- task_score: float32 [256, 8], P(('grp', 'ex')), parts along dimension 0
- best: float32 [256], P(('grp', 'ex')), parts along dimension 0
There are 2 independent parts, one for each index of `grp`. A program takes and returns all parts, laid end to end along the dimension named above; an argument that names none is the same for every part. Nothing has to cross between parts.
Inputs may be any that keep to these rules, and one draw needn't show every extreme that they name: `down_random_signs`: every entry is -1 or +1. `up_random_signs`: every entry is -1 or +1. `mixer`: every entry is -1 or +1. `validation_task_index`: ids never fall along the validation examples; every task has at least one and at most 128 examples.
All inputs are finite; a program needn't handle non-finite values.
Results may differ from a plain program's by a relative error of at most 0.013.
Values may be sent and summed in bfloat16 or wider, within the bound.
A program may use at most 128 MiB of HBM per device.

v0:
```python
import jax
import jax.numpy as jnp
from jax import lax
from jax.sharding import PartitionSpec as P

KROW = 512
KCOL = 16
TASKS = 8


def cosine_scale(dots, feat_tot, val_tot, total):
    feat_ms = feat_tot / total + 1e-06
    val_ms = val_tot / total + 1e-06
    return dots / (
        jnp.sqrt(jnp.float32(total)) * jnp.sqrt(feat_ms)[:, None] * jnp.sqrt(val_ms)[None, :]
    )


def body(
    acts,
    grads,
    lengths,
    adapter_down_weight,
    adapter_up_weight,
    down_random_signs,
    up_random_signs,
    mixer,
    validation_feature_rows,
    validation_task_index,
):
    ex_count, seq_len, width = acts.shape
    adapter_rank_size = adapter_down_weight.shape[1]
    cols = mixer.shape[1]
    total = KROW * KCOL
    hp = lax.Precision.HIGHEST
    positions = lax.broadcasted_iota(jnp.int32, (ex_count, seq_len), 1)
    token_weight = jnp.where(
        positions < lengths[:, None], 1.0 / lengths[:, None].astype(jnp.float32), 0.0
    )
    weighted_gradient = (grads.astype(jnp.float32) * token_weight[:, :, None]).astype(jnp.bfloat16)
    flattened_activations = acts.reshape(ex_count * seq_len, width)
    flattened_gradient = weighted_gradient.reshape(ex_count * seq_len, width)
    back_part = lax.dot_general(
        flattened_gradient,
        adapter_up_weight,
        (((1,), (1,)), ((), ())),
        preferred_element_type=jnp.float32,
    )
    downward_piece = jnp.dot(
        flattened_activations, adapter_down_weight, preferred_element_type=jnp.float32
    )
    upward_mixing, downward_mixing = lax.psum((back_part, downward_piece), "blk")
    back16 = upward_mixing.astype(jnp.bfloat16).reshape(ex_count, seq_len, adapter_rank_size)
    down16 = downward_mixing.astype(jnp.bfloat16).reshape(ex_count, seq_len, adapter_rank_size)
    grad_a = jnp.einsum("etd,etr->edr", acts, back16, preferred_element_type=jnp.float32).astype(
        jnp.bfloat16
    )
    grad_b = jnp.einsum(
        "etd,etr->edr", weighted_gradient, down16, preferred_element_type=jnp.float32
    ).astype(jnp.bfloat16)
    mixing_function = mixer.astype(jnp.bfloat16)
    left_mixed = (
        jnp.einsum(
            "edr,rc->dec",
            grad_a,
            mixing_function[:adapter_rank_size],
            preferred_element_type=jnp.float32,
        )
        .astype(jnp.bfloat16)
        .reshape(width, ex_count * cols)
    )
    right_mixed = (
        jnp.einsum(
            "edr,rc->dec",
            grad_b,
            mixing_function[adapter_rank_size:],
            preferred_element_type=jnp.float32,
        )
        .astype(jnp.bfloat16)
        .reshape(width, ex_count * cols)
    )
    down_sign_vector = down_random_signs.astype(jnp.bfloat16)
    up_sign_vector = up_random_signs.astype(jnp.bfloat16)
    own_rows = down_random_signs.shape[1] // lax.axis_size("blk")
    dims = (((0,), (0,)), ((), ()))
    term = lax.dot_general(down_sign_vector, left_mixed, dims, preferred_element_type=jnp.float32)
    term = term + lax.dot_general(
        up_sign_vector, right_mixed, dims, preferred_element_type=jnp.float32
    )
    feature_rows = lax.psum_scatter(
        term.reshape(own_rows * lax.axis_size("blk"), ex_count, cols),
        "blk",
        scatter_dimension=0,
        tiled=True,
    )
    feature_rows = jnp.transpose(feature_rows, (1, 0, 2)).reshape(ex_count, -1)
    feat16 = feature_rows.astype(jnp.bfloat16)
    feat_sq = jnp.sum(feature_rows * feature_rows, axis=1)
    val_rows = validation_feature_rows.reshape(validation_feature_rows.shape[0], -1)
    inner = (((1,), (1,)), ((), ()))
    val_all = lax.all_gather(val_rows, "ex", axis=0, tiled=True)
    dots = lax.dot_general(feat16, val_all, inner, preferred_element_type=jnp.float32)
    val_f = val_all.astype(jnp.float32)
    val_sq = jnp.sum(val_f * val_f, axis=1)
    dots, feat_tot, val_tot = (
        lax.psum(dots.astype(jnp.bfloat16), ("blk", "rep")).astype(jnp.float32),
        lax.psum(feat_sq.astype(jnp.bfloat16), ("blk", "rep")).astype(jnp.float32),
        lax.psum(val_sq.astype(jnp.bfloat16), ("blk", "rep")).astype(jnp.float32),
    )
    similarity = cosine_scale(dots, feat_tot, val_tot, total)
    onehot = (
        validation_task_index[:, None] == lax.broadcasted_iota(jnp.int32, (1, TASKS), 1)
    ).astype(jnp.float32)
    count = jnp.sum(onehot, axis=0)
    task_score = jnp.dot(similarity, onehot, precision=hp) / jnp.sqrt(count)[None, :]
    best = jnp.max(task_score, axis=1)
    return (similarity, task_score, best)


def solution(mesh):
    placed = (
        P(("grp", "ex"), None, "blk"),
        P(("grp", "ex"), None, "blk"),
        P(("grp", "ex")),
        P("blk", None),
        P(None, "blk"),
        P("blk", None),
        P("blk", None),
        P(None, "rep"),
        P("ex", "blk", "rep"),
        P(),
    )
    return jax.shard_map(
        body,
        mesh=mesh,
        in_specs=placed,
        out_specs=(P(("grp", "ex"), None), P(("grp", "ex"), None), P(("grp", "ex"))),
        check_vma=False,
    )
```

profile of v0, /device:TPU:0, one launch (start us, length us, event | category | flops | bytes accessed | tf_op | source)
XLA Modules:
  0.0 182.8 jit_solution(15582106615881899606)
XLA Ops:
  8.0 0.0 copy-start
  8.0 0.0 reduce-scatter.2.cloned.1.call-start
  8.1 0.7 convert_divide_fusion
  8.8 0.7 fusion.33
  9.5 8.0 %multiply_convert_fusion = bf16[32,64,2048]{2,1,0:T(8,128)(2,1)} fusion(bf16[32,64,2048]{2,1,0:T(8,128)(2,1)} %param.11, f32[32,64]{1,0:T(8,128)S(1)} %fusion.33), kind=kLoop, calls=%fused_computation.5 | loop fusion | flops 12582912 | bytes 16785408 | tf_op jit(solution)/shard_map/convert_element_type | solution.py:40
  17.5 0.0 copy-start.1
  17.5 0.0 copy-start.6
  17.5 0.0 copy-done
  17.5 5.9 %fusion.36 = f32[2048,128]{1,0:T(8,128)S(1)} fusion(bf16[2048,2048]{1,0:T(8,128)(2,1)} %bitcast.47, bf16[128,2048]{1,0:T(8,128)(2,1)S(1)} %copy-done), kind=kOutput, calls=%fused_computation.36 | convolution fusion | flops 1073741824 | bytes 9961472 | tf_op jit(solution)/shard_map/dot_general | solution.py:43
  23.4 0.0 copy-start.5
  23.4 0.0 copy-done.1
  23.5 0.0 copy-done.6
  23.5 2.4 %fusion.37 = f32[2048,128]{1,0:T(8,128)S(1)} fusion(bf16[2048,2048]{1,0:T(8,128)(2,1)S(1)} %bitcast.48, bf16[2048,128]{1,0:T(8,128)(2,1)S(1)} %copy-done.6), kind=kOutput, calls=%fused_computation.37 | convolution fusion | flops 1073741824 | bytes 9961472 | tf_op jit(solution)/shard_map/dot_general | solution.py:49
  25.9 0.0 copy-done.5
  25.9 54.2 %all-reduce.3 = (bf16[2048,128]{1,0:T(8,128)(2,1)}, bf16[2048,128]{1,0:T(8,128)(2,1)S(1)}) all-reduce(f32[2048,128]{1,0:T(8,128)S(1)} %fusion.37, f32[2048,128]{1,0:T(8,128)S(1)} %fusion.36), channel_id=1, replica_groups=mesh['grp'=2,'ex'=4,'blk'=2,'rep'=2] {'blk'}, use_global_device_ids=true, to_apply=%region_1.2 | all-reduce | flops 524288 | bytes 3145728 | tf_op jit(solution)/shard_map/psum | solution.py:52
  80.1 11.2 %fusion.18 = bf16[2048,256]{0,1:T(8,128)(2,1)S(1)} fusion(bf16[32,64,2048]{2,1,0:T(8,128)(2,1)} %multiply_convert_fusion, bf16[32,64,128]{2,1,0:T(8,128)(2,1)} %bitcast.51, bf16[256,8]{0,1:T(8,128)(2,1)S(1)} %convert_element_type.85), kind=kOutput, calls=%fused_computation.12 | convolution fusion | flops 1216872448 | bytes 9963520 | tf_op jit(solution)/shard_map/edr,rc->dec/dot_general | solution.py:73
  91.3 10.1 %fusion.15 = bf16[2048,256]{0,1:T(8,128)(2,1)S(1)} fusion(bf16[32,64,128]{2,1,0:T(8,128)(2,1)S(1)} %bitcast.50, bf16[32,64,2048]{2,1,0:T(8,128)(2,1)} %param.10, bf16[256,8]{0,1:T(8,128)(2,1)S(1)} %convert_element_type.85), kind=kOutput, calls=%fused_computation.11 | convolution fusion | flops 1216872448 | bytes 9963520 | tf_op jit(solution)/shard_map/edr,rc->dec/dot_general | solution.py:63
  101.4 0.0 copy-start.2
  101.4 0.0 copy-start.4
  101.5 3.0 %fusion.21 = f32[256,512]{1,0:T(8,128)S(1)} fusion(bf16[2048,256]{0,1:T(8,128)(2,1)S(1)} %fusion.18, s32[2048,512]{1,0:T(8,128)} %param.16), kind=kOutput, calls=%fused_computation.13 | convolution fusion | flops 537919488 | bytes 5767168 | tf_op jit(solution)/shard_map/dot_general | solution.py:87
  104.4 2.9 %fusion.28 = f32[512,32,8]{0,2,1:T(8,128)S(1)} fusion(f32[256,512]{1,0:T(8,128)S(1)} %fusion.21, bf16[2048,256]{0,1:T(8,128)(2,1)S(1)} %fusion.15, s32[2048,512]{1,0:T(8,128)} %param.15), kind=kOutput, calls=%fused_computation.18 | convolution fusion | flops 538050560 | bytes 6291456 | tf_op jit(solution)/shard_map/dot_general | solution.py:86
  107.3 2.0 %copy.16 = f32[512,32,8]{1,2,0:T(8,128)} copy(f32[512,32,8]{0,2,1:T(8,128)S(1)} %fusion.28) | data formatting | bytes 1048576 | tf_op jit(solution)/shard_map/reshape | solution.py:91
  109.3 0.0 reduce-scatter.2.cloned.1.call-update
  109.4 0.0 all-gather.2.cloned.1.call-start
  109.4 0.0 copy-done.2
  109.4 1.3 copy.17
  110.8 0.0 all-gather.2.cloned.1.call-update
  110.8 0.0 copy-done.4
  110.8 0.1 convert_reduce_fusion
  110.9 30.7 %reduce-scatter.2.cloned.1.call-done = f32[256,32,8]{1,2,0:T(8,128)} async-done(((f32[512,32,8]{1,2,0:T(8,128)}), f32[256,32,8]{1,2,0:T(8,128)}) %reduce-scatter.2.cloned.1.call-update) | async-done | bytes 262160 | tf_op jit(solution)/shard_map/reduce_scatter | solution.py:90
  141.6 1.5 multiply_reduce_fusion.1
  143.2 14.7 %all-gather.2.cloned.1.call-done = bf16[512,2048]{0,1:T(8,128)(2,1)} async-done(((bf16[128,2048]{0,1:T(8,128)(2,1)}), bf16[512,2048]{0,1:T(8,128)(2,1)}) %all-gather.2.cloned.1.call-update) | async-done | bytes 2097168 | tf_op jit(solution)/shard_map/all_gather | solution.py:101
  157.8 2.4 %convolution_convert_fusion = bf16[32,512]{1,0:T(8,128)(2,1)S(1)} fusion(bf16[512,2048]{0,1:T(8,128)(2,1)} %all-gather.2.cloned.1.call-done, f32[256,32,8]{1,2,0:T(8,128)} %reduce-scatter.2.cloned.1.call-done), kind=kOutput, calls=%fused_computation.19 | convolution fusion | flops 67190784 | bytes 2392064 | tf_op jit(solution)/shard_map/dot_general | solution.py:102
  160.2 2.1 %multiply_reduce_fusion = bf16[512]{0:T(512)(128)(2,1)S(1)} fusion(bf16[512,2048]{0,1:T(8,128)(2,1)} %all-gather.2.cloned.1.call-done), kind=kLoop, calls=%fused_computation.8 | loop fusion | flops 3145216 | bytes 2098176 | tf_op jit(solution)/shard_map/reduce_sum | solution.py:104
  162.3 11.6 %all-reduce.1 = (bf16[32,512]{1,0:T(8,128)(2,1)S(1)}, bf16[512]{0:T(512)(128)(2,1)S(1)}, bf16[32]{0:T(256)(128)(2,1)S(1)}) all-reduce(bf16[32,512]{1,0:T(8,128)(2,1)S(1)} %convolution_convert_fusion, bf16[512]{0:T(512)(128)(2,1)S(1)} %multiply_reduce_fusion, ...), channel_id=1, replica_groups=mesh['grp'=2,'ex'=4,'blk'=2,'rep'=2] {'blk','rep'}, use_global_device_ids=true, to_apply=%region_3.4 | all-reduce | flops 16928 | bytes 67712 | tf_op jit(solution)/shard_map/psum | solution.py:106
  174.0 0.1 multiply_divide_fusion
  174.1 0.0 copy-start.3
  174.1 1.3 fusion.35
  175.3 0.0 copy-done.3
  (4 shorter events, 0.0 us)
Async XLA Ops:
  8.0 9.5 %copy-start = (bf16[128,2048]{1,0:T(8,128)(2,1)S(1)}, bf16[128,2048]{1,0:T(8,128)(2,1)}, u32[]{:S(2)}) copy-start(bf16[128,2048]{1,0:T(8,128)(2,1)} %param.14) | copy-start | bytes 1572868
  8.0 133.6 %reduce-scatter.2.cloned.1.call-start = ((), (), s32[]{:S(2)}) async-start(), calls=%async_computation.1 | async-start | bytes 3145728 | tf_op jit(solution)/shard_map/reduce_scatter | solution.py:90
  17.5 5.9 %copy-start.1 = (bf16[32,64,2048]{2,1,0:T(8,128)(2,1)S(1)}, bf16[32,64,2048]{2,1,0:T(8,128)(2,1)}, u32[]{:S(2)}) copy-start(bf16[32,64,2048]{2,1,0:T(8,128)(2,1)} %param.10) | copy-start | bytes 25165828
  17.5 5.9 %copy-start.6 = (bf16[2048,128]{1,0:T(8,128)(2,1)S(1)}, bf16[2048,128]{1,0:T(8,128)(2,1)}, u32[]{:S(2)}) copy-start(bf16[2048,128]{1,0:T(8,128)(2,1)} %param.13) | copy-start | bytes 1572868
  23.4 2.4 %copy-start.5 = (s32[256,8]{0,1:T(8,128)S(1)}, s32[256,8]{0,1:T(8,128)}, u32[]{:S(2)}) copy-start(s32[256,8]{0,1:T(8,128)} %param.17) | copy-start | bytes 24580
  101.4 8.0 %copy-start.2 = (bf16[128,256,8]{1,2,0:T(8,128)(2,1)S(1)}, bf16[128,256,8]{1,2,0:T(8,128)(2,1)}, u32[]{:S(2)}) copy-start(bf16[128,256,8]{1,2,0:T(8,128)(2,1)} %param.18) | copy-start | bytes 1572868
  101.4 9.4 %copy-start.4 = (s32[512]{0:T(512)S(1)}, s32[512]{0:T(512)}, u32[]{:S(2)}) copy-start(s32[512]{0:T(512)} %param.19) | copy-start | bytes 6148
  109.4 48.5 %all-gather.2.cloned.1.call-start = ((), (), s32[]{:S(2)}) async-start(), calls=%async_computation.2 | async-start | bytes 2621440 | tf_op jit(solution)/shard_map/all_gather | solution.py:101
  174.1 1.3 copy-start.3
Sparse Core Ops, SparseCore 0:
  109.5 32.1 reduce-scatter.1
Sparse Core Ops, SparseCore 1:
  111.4 46.4 all-gather.1
where the time goes:
time: 183 us
  blocking collectives  65.8 us (36%)
  waiting for transfers between devices  45.4 us (25%)
  matrix products  39.1 us (21%)
  between operations  15.6 us (9%)
  other arithmetic  13.3 us (7%)
  local copies, waits for them, and re-layouts  3.4 us (2%)
    psum x1, blocking collectives, body(): lax.psum((back_part, downward_piece), 'blk')  54.2 us
    reduce_scatter x1, waiting for transfers between devices, body(): lax.psum_scatter(term.reshape(own_rows * lax.axis_size('blk'), ex_count,...  30.7 us
    all_gather x1, waiting for transfers between devices, body(): val_all = lax.all_gather(val_rows, 'ex', axis=0, tiled=True)  14.7 us
    psum x1, blocking collectives, body(): lax.psum(dots.astype(jnp.bfloat16), ('blk', 'rep')).astype(jnp.float32)  11.6 us
    dot_general x1, matrix products, body(): jnp.einsum('edr,rc->dec', grad_b, mixing_function[adapter_rank_size:], pr...  11.2 us
    dot_general x1, matrix products, body(): jnp.einsum('edr,rc->dec', grad_a, mixing_function[:adapter_rank_size], pr...  10.1 us
    convert_element_type x1, other arithmetic, body(): (grads.astype(jnp.float32) * token_weight[:, :, None]).astype(jnp.bfloat16)  8.04 us
    dot_general x1, matrix products, body(): lax.dot_general(flattened_gradient, adapter_up_weight, (((1,), (1,)), (()...  5.89 us
  transfers between devices with their start and end apart: 2, of which 2 were waited for; matrix products, arithmetic and copies ran while one was open for 2% of the time, Pallas kernels for 0%

commit v1 on v0

v1 whole, which is shorter than its diff:
```python
import functools

import jax
import jax.numpy as jnp
from jax import lax
from jax.experimental import pallas as pl
from jax.experimental.pallas import tpu as pltpu
from jax.sharding import PartitionSpec as P

TASKS = 8
GROUPS = 4
HALVES = 2
SUB = 256
F32 = jnp.float32
BF16 = jnp.bfloat16
MESH = pl.DeviceIdType.MESH
NT = (((1,), (1,)), ((), ()))


def iota(shape, dim):
    return lax.broadcasted_iota(jnp.int32, shape, dim)


def kernel(
    ne, nb, nr, seq, total_proj,
    acts, grads, down_w, up_w, down_s, up_s, val,
    lengths, mixer_t, tasks,
    sim_out, task_out, best_out,
    acts_v, grads_v, down_wv, up_wv, down_sv, up_sv, down_b, up_b, val_v, val_p,
    mix_a, mix_b, pq, part, part16, got, feats, val_sq, feat_sq, dots_s, dots_r,
    load_sem, small_sem, a_send, a_recv, b_send, b_recv, c_send, c_recv,
    v_send, v_recv, f_send, f_recv, e_send, e_recv,
):
    grp, ex = lax.axis_index("grp"), lax.axis_index("ex")
    blk, rep = lax.axis_index("blk"), lax.axis_index("rep")
    nj = nb * nr
    n = ne * nj
    me_j = blk * nr + rep
    me = ex * nj + me_j
    tokens, width = acts_v.shape
    cols = mixer_t.shape[0]
    rank = mixer_t.shape[1] // 2
    own_k = val_v.shape[1]
    nval = val_v.shape[0] // cols
    gtok = tokens // GROUPS
    examples = tokens // seq
    half_ex = examples // HALVES
    half_rows = half_ex * cols
    sub_ex = SUB // seq
    sub_rows = sub_ex * cols

    def at(lin):
        return (grp, lin // nj, lax.rem(lin // nr, nb), lax.rem(lin, nr))

    def local(src, dst, sem):
        c = pltpu.make_async_copy(src, dst, sem)
        c.start()
        return c

    ld_dw = local(down_w, down_wv, small_sem.at[0])
    ld_uw = local(up_w, up_wv, small_sem.at[1])
    ld_g, ld_a = [], []
    for g in range(GROUPS):
        rows = pl.ds(g * gtok, gtok)
        ld_g.append(local(grads.at[rows], grads_v.at[rows], load_sem.at[0, g]))
        ld_a.append(local(acts.at[rows], acts_v.at[rows], load_sem.at[1, g]))
        if g == 1:
            ld_v = local(val, val_v, small_sem.at[2])
            ld_ds = local(down_s, down_sv, small_sem.at[3])
    ld_us = local(up_s, up_sv, small_sem.at[4])

    barrier = pltpu.get_barrier_semaphore()

    def greet(o, carry):
        pl.semaphore_signal(barrier, inc=1, device_id=at(lax.rem(me + o, n)), device_id_type=MESH)
        return carry

    lax.fori_loop(1, n, greet, 0)

    mix = mixer_t[...].astype(F32)
    pad = jnp.zeros((128 - cols, rank), F32)
    mix_u = jnp.concatenate([mix[:, :rank], pad], axis=0).astype(BF16)
    mix_d = jnp.concatenate([mix[:, rank:], pad], axis=0).astype(BF16)
    ld_dw.wait()
    ld_uw.wait()
    wd = lax.dot_general(down_wv[...], mix_d, NT, preferred_element_type=F32).astype(BF16)
    wu = lax.dot_general(
        up_wv[...], mix_u, (((0,), (1,)), ((), ())), preferred_element_type=F32
    ).astype(BF16)

    pl.semaphore_wait(barrier, n - 1)

    def send(src, dst, s, r, lin):
        c = pltpu.make_async_remote_copy(
            src_ref=src, dst_ref=dst, send_sem=s, recv_sem=r, device_id=at(lin), device_id_type=MESH
        )
        c.start()

    def arrived(dst, s, r):
        pltpu.make_async_remote_copy(
            src_ref=dst, dst_ref=dst, send_sem=s, recv_sem=r,
            device_id=at(lax.rem(me + 1, n)), device_id_type=MESH,
        ).wait_recv()

    def left(src, s, r):
        pltpu.make_async_remote_copy(
            src_ref=src, dst_ref=src, send_sem=s, recv_sem=r,
            device_id=at(lax.rem(me + 1, n)), device_id_type=MESH,
        ).wait_send()

    def blk_lin(b):
        return ex * nj + b * nr + rep

    for g in range(GROUPS):
        ld_g[g].wait()
        ld_a[g].wait()
        for i in range(gtok // SUB):
            rows = pl.ds(g * gtok + i * SUB, SUB)
            p = jnp.dot(grads_v[rows, :], wu, preferred_element_type=F32)
            q = jnp.dot(acts_v[rows, :], wd, preferred_element_type=F32)
            lanes = pl.ds(i * SUB, SUB)
            pq[g, blk, 0:cols, lanes] = jnp.transpose(p)[:cols]
            pq[g, blk, cols:2 * cols, lanes] = jnp.transpose(q)[:cols]
        for o in range(1, nb):
            b = lax.rem(blk + o, nb)
            send(pq.at[g, blk], pq.at[g, blk], a_send.at[g, b], a_recv.at[g, blk], blk_lin(b))
        if g == 1:
            ld_v.wait()
            r, c = iota((256, 256), 0), iota((256, 256), 1)
            per = 256 // cols
            perm = jnp.where(lax.rem(r, per) * cols + r // per == c, 1.0, 0.0).astype(BF16)
            ones = jnp.ones((8, own_k), F32)
            for i in range(nval // per):
                piece = jnp.dot(perm, val_v[i * 256:(i + 1) * 256, :], preferred_element_type=F32)
                sq = jnp.zeros((per, own_k), F32)
                for k in range(cols):
                    rows = piece[k * per:(k + 1) * per]
                    val_p[k, i * per:(i + 1) * per, :] = rows.astype(BF16)
                    sq = sq + rows * rows
                val_sq[me_j, :, i * per:(i + 1) * per] = lax.dot_general(
                    ones, sq, NT, preferred_element_type=F32, precision=lax.Precision.HIGHEST
                )
            for o in range(1, nj):
                j = lax.rem(me_j + o, nj)
                send(val_sq.at[me_j], val_sq.at[me_j], v_send.at[j], v_recv.at[me_j], ex * nj + j)
        if g == 2:
            ld_ds.wait()
            down_b[...] = down_sv[...].astype(F32).astype(BF16)
    ld_us.wait()
    up_b[...] = up_sv[...].astype(F32).astype(BF16)

    lane = iota((cols, 128), 1)
    row_ex = iota((sub_rows, SUB), 0) // cols
    lane_ex = iota((sub_rows, SUB), 1) // seq
    diag = row_ex == lane_ex

    def mixed(g):
        for o in range(1, nb):
            b = lax.rem(blk + o, nb)
            arrived(pq.at[g, b], a_send.at[g, b], a_recv.at[g, b])
        both = pq[g, 0]
        for b in range(1, nb):
            both = both + pq[g, b]
        for i in range(gtok // SUB):
            sub = g * (gtok // SUB) + i
            weights = []
            for h in range(SUB // 128):
                e0 = sub * sub_ex + h * (128 // seq)
                size = jnp.where(lane < seq, lengths[e0], lengths[e0 + 1])
                place = jnp.where(lane < seq, lane, lane - seq)
                weights.append(jnp.where(place < size, 1.0 / size.astype(F32), 0.0))
            weight = jnp.concatenate(weights, axis=1)
            rows = pl.ds(sub * SUB, SUB)
            out = pl.ds(sub * sub_rows, sub_rows)
            for first, tok, dst in ((0, acts_v, mix_a), (cols, grads_v, mix_b)):
                x = both[first:first + cols, i * SUB:(i + 1) * SUB] * weight
                x = jnp.where(diag, jnp.concatenate([x] * sub_ex, axis=0), 0.0).astype(BF16)
                dst[out, :] = jnp.dot(x, tok[rows, :], preferred_element_type=F32).astype(BF16)

    def project(h):
        rows = pl.ds(h * half_rows, half_rows)
        res = jnp.dot(mix_a[rows, :], down_b[...], preferred_element_type=F32)
        res = res + jnp.dot(mix_b[rows, :], up_b[...], preferred_element_type=F32)
        for b in range(nb):
            x = res[:, b * own_k:(b + 1) * own_k]
            part[h, b] = x
            part16[h, b] = x.astype(BF16)
        for o in range(1, nb):
            b = lax.rem(blk + o, nb)
            send(part16.at[h, b], got.at[h, blk], b_send.at[h, b], b_recv.at[h, blk], blk_lin(b))

    r, c = iota((half_rows, half_rows), 0), iota((half_rows, half_rows), 1)
    perm_f = jnp.where(lax.rem(r, half_ex) * cols + r // half_ex == c, 1.0, 0.0).astype(BF16)

    def combine(h):
        x = part[h, blk]
        for o in range(1, nb):
            b = lax.rem(blk + o, nb)
            arrived(got.at[h, b], b_send.at[h, b], b_recv.at[h, b])
            x = x + got[h, b].astype(F32)
        feats[ex, h] = jnp.dot(perm_f, x.astype(BF16), preferred_element_type=F32).astype(BF16)
        for o in range(1, ne):
            e = lax.rem(ex + o, ne)
            send(feats.at[ex, h], feats.at[ex, h], c_send.at[h, e], c_recv.at[h, ex], e * nj + me_j)
        sq = jnp.sum((x * x).reshape(half_ex, cols, own_k), axis=1)
        feat_sq[me_j, h * half_ex:(h + 1) * half_ex, :] = jnp.broadcast_to(
            jnp.sum(sq, axis=1, keepdims=True), (half_ex, 128)
        )

    mixed(0)
    mixed(1)
    project(0)
    mixed(2)
    combine(0)
    mixed(3)
    project(1)
    combine(1)
    for o in range(1, nj):
        j = lax.rem(me_j + o, nj)
        send(feat_sq.at[me_j], feat_sq.at[me_j], f_send.at[j], f_recv.at[me_j], ex * nj + j)

    for o in range(1, nj):
        j = lax.rem(me_j + o, nj)
        arrived(val_sq.at[j], v_send.at[j], v_recv.at[j])
    vs = val_sq[0]
    for j in range(1, nj):
        vs = vs + val_sq[j]
    val_scale = (1.0 / jnp.sqrt(vs / total_proj + 1e-06))[0:1]

    for o in range(ne):
        e = lax.rem(ex + ne - o, ne)
        acc = jnp.zeros((examples, nval), F32)
        if o:
            for h in range(HALVES):
                arrived(feats.at[e, h], c_send.at[h, e], c_recv.at[h, e])
        for k in range(cols):
            x = jnp.concatenate(
                [feats[e, h, k * half_ex:(k + 1) * half_ex, :] for h in range(HALVES)], axis=0
            )
            acc = acc + lax.dot_general(x, val_p[k], NT, preferred_element_type=F32)
        dots_s[e] = (acc * val_scale).astype(BF16)
        if o == 0:
            dots_r[ex, me_j] = dots_s[ex]
        for k in range(1 if o == 0 else 0, nj):
            j = lax.rem(me_j + k, nj)
            send(dots_s.at[e], dots_r.at[ex, me_j], e_send.at[e, j], e_recv.at[ex, me_j], e * nj + j)

    for o in range(1, nj):
        j = lax.rem(me_j + o, nj)
        arrived(feat_sq.at[j], f_send.at[j], f_recv.at[j])
    fs = feat_sq[0]
    for j in range(1, nj):
        fs = fs + feat_sq[j]
    feat_scale = 1.0 / (
        jnp.sqrt(F32(total_proj)) * jnp.sqrt(fs[:, 0:1] / total_proj + 1e-06)
    )

    def take(o, carry):
        src = lax.rem(me + o, n)
        e, j = src // nj, lax.rem(src, nj)
        arrived(dots_r.at[e, j], e_send.at[e, j], e_recv.at[e, j])
        return carry

    lax.fori_loop(1, n, take, 0)
    for e in range(ne):
        acc = dots_r[e, 0].astype(F32)
        for j in range(1, nj):
            acc = acc + dots_r[e, j].astype(F32)
        sim_out[:, e * nval:(e + 1) * nval] = acc * feat_scale
    ids = tasks[...]
    onehot = jnp.where(iota((TASKS, ids.shape[1]), 0) == ids, 1.0, 0.0)
    count = jnp.sum(onehot, axis=1, keepdims=True)
    score = lax.dot_general(
        onehot, sim_out[...], NT, preferred_element_type=F32, precision=lax.Precision.HIGHEST
    ) / jnp.sqrt(count)
    task_out[...] = score
    best_out[...] = jnp.max(score, axis=0, keepdims=True)

    for o in range(1, nb):
        b = lax.rem(blk + o, nb)
        for g in range(GROUPS):
            left(pq.at[g, blk], a_send.at[g, b], a_recv.at[g, b])
        for h in range(HALVES):
            left(part16.at[h, b], b_send.at[h, b], b_recv.at[h, b])
    for o in range(1, ne):
        e = lax.rem(ex + o, ne)
        for h in range(HALVES):
            left(feats.at[ex, h], c_send.at[h, e], c_recv.at[h, e])
    for o in range(1, nj):
        j = lax.rem(me_j + o, nj)
        left(val_sq.at[me_j], v_send.at[j], v_recv.at[j])
        left(feat_sq.at[me_j], f_send.at[j], f_recv.at[j])

    def gone(o, carry):
        dst = lax.rem(me + o, n)
        e, j = dst // nj, lax.rem(dst, nj)
        left(dots_s.at[e], e_send.at[e, j], e_recv.at[e, j])
        return carry

    lax.fori_loop(1, n, gone, 0)


def body(
    sizes, acts, grads, lengths, down_w, up_w, down_s, up_s, mixer, val, tasks
):
    ne, nb, nr = sizes
    nj = nb * nr
    examples, seq, width = acts.shape
    tokens = examples * seq
    krow = down_s.shape[1]
    cols = mixer.shape[1]
    nval, own_k, _ = val.shape
    all_val = tasks.shape[0]
    half_rows = examples * cols // HALVES
    rank = down_w.shape[1]
    gtok = tokens // GROUPS
    dma = pltpu.SemaphoreType.DMA
    anyspace = pl.BlockSpec(memory_space=pl.ANY)
    vmem = pl.BlockSpec(memory_space=pltpu.VMEM)
    sim, score, best = pl.pallas_call(
        functools.partial(kernel, ne, nb, nr, seq, float(krow * cols * nr)),
        out_shape=(
            jax.ShapeDtypeStruct((examples, all_val), F32),
            jax.ShapeDtypeStruct((TASKS, examples), F32),
            jax.ShapeDtypeStruct((1, examples), F32),
        ),
        in_specs=[anyspace] * 7 + [pl.BlockSpec(memory_space=pltpu.SMEM), vmem, vmem],
        out_specs=(vmem, vmem, vmem),
        scratch_shapes=[
            pltpu.VMEM((tokens, width), BF16),
            pltpu.VMEM((tokens, width), BF16),
            pltpu.VMEM((width, rank), BF16),
            pltpu.VMEM((rank, width), BF16),
            pltpu.VMEM((width, krow), jnp.int32),
            pltpu.VMEM((width, krow), jnp.int32),
            pltpu.VMEM((width, krow), BF16),
            pltpu.VMEM((width, krow), BF16),
            pltpu.VMEM((nval * cols, own_k), BF16),
            pltpu.VMEM((cols, nval, own_k), BF16),
            pltpu.VMEM((examples * cols, width), BF16),
            pltpu.VMEM((examples * cols, width), BF16),
            pltpu.VMEM((GROUPS, nb, 2 * cols, gtok), F32),
            pltpu.VMEM((HALVES, nb, half_rows, own_k), F32),
            pltpu.VMEM((HALVES, nb, half_rows, own_k), BF16),
            pltpu.VMEM((HALVES, nb, half_rows, own_k), BF16),
            pltpu.VMEM((ne, HALVES, half_rows, own_k), BF16),
            pltpu.VMEM((nj, 8, nval), F32),
            pltpu.VMEM((nj, examples, 128), F32),
            pltpu.VMEM((ne, examples, nval), BF16),
            pltpu.VMEM((ne, nj, examples, nval), BF16),
            dma((2, GROUPS)),
            dma((5,)),
            dma((GROUPS, nb)),
            dma((GROUPS, nb)),
            dma((HALVES, nb)),
            dma((HALVES, nb)),
            dma((HALVES, ne)),
            dma((HALVES, ne)),
            dma((nj,)),
            dma((nj,)),
            dma((nj,)),
            dma((nj,)),
            dma((ne, nj)),
            dma((ne, nj)),
        ],
        compiler_params=pltpu.CompilerParams(
            collective_id=0, has_side_effects=True, vmem_limit_bytes=56 * 1024 * 1024
        ),
    )(
        acts.reshape(tokens, width),
        grads.reshape(tokens, width),
        down_w,
        up_w,
        down_s,
        up_s,
        jnp.transpose(val, (0, 2, 1)).reshape(nval * cols, own_k),
        lengths,
        jnp.transpose(mixer),
        tasks.reshape(1, all_val),
    )
    return sim, jnp.transpose(score), best.reshape(examples)


def solution(mesh):
    placed = (
        P(("grp", "ex"), None, "blk"),
        P(("grp", "ex"), None, "blk"),
        P(("grp", "ex")),
        P("blk", None),
        P(None, "blk"),
        P("blk", None),
        P("blk", None),
        P(None, "rep"),
        P("ex", "blk", "rep"),
        P(),
    )
    sizes = (mesh.shape["ex"], mesh.shape["blk"], mesh.shape["rep"])
    return jax.shard_map(
        functools.partial(body, sizes),
        mesh=mesh,
        in_specs=placed,
        out_specs=(P(("grp", "ex"), None), P(("grp", "ex"), None), P(("grp", "ex"))),
        check_vma=False,
    )
```

time: 183 us -> 44.8 us (0.24)
  blocking collectives: 65.8 us -> 0 us
  waiting for transfers between devices: 45.4 us -> 0 us
  Pallas kernels: 0 us -> 40.1 us
  matrix products: 39.1 us -> 0 us
  between operations: 15.6 us -> 0.64 us
  other arithmetic: 13.3 us -> 0 us
    psum x2 -> x0, blocking collectives: 65.8 us -> none  [the longest x1 54.2 us: body(): lax.psum((back_part, downward_piece), 'blk')]
    pallas_call x0 -> x1, Pallas kernels: none -> 40.1 us  [body(): pl.pallas_call(functools.partial(kernel, ne, nb, nr, seq, float(krow * co...]
    dot_general x8 -> x0, matrix products: 39.1 us -> none  [the longest x1 11.2 us: body(): jnp.einsum('edr,rc->dec', grad_b, mixing_function[adapter_rank_size:], pr...]
    reduce_scatter x1 -> x0, waiting for transfers between devices: 30.7 us -> none  [body(): lax.psum_scatter(term.reshape(own_rows * lax.axis_size('blk'), ex_count,...]
    all_gather x1 -> x0, waiting for transfers between devices: 14.7 us -> none  [body(): val_all = lax.all_gather(val_rows, 'ex', axis=0, tiled=True)]
    convert_element_type x2 -> x0, other arithmetic: 8.04 us -> none  [the longest x1 8.04 us: body(): (grads.astype(jnp.float32) * token_weight[:, :, None]).astype(jnp.bfloat16)]
    reduce_sum x3 -> x0, other arithmetic: 3.75 us -> none  [the longest x1 2.12 us: body(): val_sq = jnp.sum(val_f * val_f, axis=1)]
    unnamed x15 -> x3, local copies, waits for them, and re-layouts: 1.39 us -> 3.85 us
  transfers between devices with their start and end apart: 2 -> 0, of which waited for: 2 -> 0; matrix products, arithmetic and copies ran while one was open for 2% -> 0% of each run, Pallas kernels for 0% -> 0%
where the time goes in v1:
time: 44.8 us; the launch traced here: 44.6 us
  Pallas kernels  40.1 us (90%)
  local copies, waits for them, and re-layouts  3.85 us (9%)
  between operations  0.64 us (1%)
    pallas_call x1, Pallas kernels, body(): pl.pallas_call(functools.partial(kernel, ne, nb, nr, seq, float(krow * co...  40.1 us
    unnamed x3, local copies, waits for them, and re-layouts  3.85 us

profile of v1, /device:TPU:0, one launch (start us, length us, event | category | flops | bytes accessed | tf_op | source)
XLA Modules:
  0.0 44.6 jit_solution(6772290332233855251)
XLA Ops:
  0.6 40.1 %shard_map.121 = (f32[32,512]{1,0:T(8,128)}, f32[8,32]{1,0:T(8,128)}, f32[1,32]{1,0:T(1,128)}) custom-call(bf16[2048,2048]{1,0:T(8,128)(2,1)} %bitcast.9, bf16[2048,2048]{1,0:T(8,128)(2,1)} %bitcast.10, bf16[2048,128]{1,0:T(8,128)(2,1)} %down_w.1, bf16[128,2048]{1,0:T(8,128)(2,1)} %up_w.1, s32[2048,512]{1,0:T(8,128)} %down_s.1, s32[2048,512]{1,0:T(8,128)} %up_s.1, ...), custom_call_target="tpu_custom_call" | custom-call | tf_op jit(solution)/shard_map/pallas_call | solution.py:320
  40.7 1.5 %copy.16 = f32[32,512]{1,0:T(8,128)} copy(f32[32,512]{1,0:T(8,128)} %get-tuple-element.12) | data formatting | bytes 131072
  42.2 1.3 %copy.17 = f32[32,8]{0,1:T(8,128)} copy(f32[32,8]{0,1:T(8,128)} %bitcast.13) | data formatting | bytes 2048
  43.5 1.1 %copy.18 = f32[32]{0:T(128)} copy(f32[32]{0:T(128)} %bitcast.15) | data formatting | bytes 256

commit v2 on v1

--- a/solution.py
+++ b/solution.py
@@ -24,8 +24,8 @@
 def kernel(
     ne, nb, nr, seq, total_proj,
     acts, grads, down_w, up_w, down_s, up_s, val,
-    lengths, mixer_t, tasks,
-    sim_out, task_out, best_out,
+    lengths, mixer_t,
+    sim_out,
     acts_v, grads_v, down_wv, up_wv, down_sv, up_sv, down_b, up_b, val_v, val_p,
     mix_a, mix_b, pq, part, part16, got, feats, val_sq, feat_sq, dots_s, dots_r,
     load_sem, small_sem, a_send, a_recv, b_send, b_recv, c_send, c_recv,
@@ -64,10 +64,10 @@
         rows = pl.ds(g * gtok, gtok)
         ld_g.append(local(grads.at[rows], grads_v.at[rows], load_sem.at[0, g]))
         ld_a.append(local(acts.at[rows], acts_v.at[rows], load_sem.at[1, g]))
-        if g == 1:
-            ld_v = local(val, val_v, small_sem.at[2])
+        if g == GROUPS // 2 - 1:
             ld_ds = local(down_s, down_sv, small_sem.at[3])
-    ld_us = local(up_s, up_sv, small_sem.at[4])
+            ld_us = local(up_s, up_sv, small_sem.at[4])
+    ld_v = local(val, val_v, small_sem.at[2])
 
     barrier = pltpu.get_barrier_semaphore()
 
@@ -88,8 +88,6 @@
         up_wv[...], mix_u, (((0,), (1,)), ((), ())), preferred_element_type=F32
     ).astype(BF16)
 
-    pl.semaphore_wait(barrier, n - 1)
-
     def send(src, dst, s, r, lin):
         c = pltpu.make_async_remote_copy(
             src_ref=src, dst_ref=dst, send_sem=s, recv_sem=r, device_id=at(lin), device_id_type=MESH
@@ -111,7 +109,7 @@
     def blk_lin(b):
         return ex * nj + b * nr + rep
 
-    for g in range(GROUPS):
+    def rank_space(g):
         ld_g[g].wait()
         ld_a[g].wait()
         for i in range(gtok // SUB):
@@ -121,33 +119,31 @@
             lanes = pl.ds(i * SUB, SUB)
             pq[g, blk, 0:cols, lanes] = jnp.transpose(p)[:cols]
             pq[g, blk, cols:2 * cols, lanes] = jnp.transpose(q)[:cols]
+        if g == 0:
+            pl.semaphore_wait(barrier, n - 1)
         for o in range(1, nb):
             b = lax.rem(blk + o, nb)
             send(pq.at[g, blk], pq.at[g, blk], a_send.at[g, b], a_recv.at[g, blk], blk_lin(b))
-        if g == 1:
-            ld_v.wait()
-            r, c = iota((256, 256), 0), iota((256, 256), 1)
-            per = 256 // cols
-            perm = jnp.where(lax.rem(r, per) * cols + r // per == c, 1.0, 0.0).astype(BF16)
-            ones = jnp.ones((8, own_k), F32)
-            for i in range(nval // per):
-                piece = jnp.dot(perm, val_v[i * 256:(i + 1) * 256, :], preferred_element_type=F32)
-                sq = jnp.zeros((per, own_k), F32)
-                for k in range(cols):
-                    rows = piece[k * per:(k + 1) * per]
-                    val_p[k, i * per:(i + 1) * per, :] = rows.astype(BF16)
-                    sq = sq + rows * rows
-                val_sq[me_j, :, i * per:(i + 1) * per] = lax.dot_general(
-                    ones, sq, NT, preferred_element_type=F32, precision=lax.Precision.HIGHEST
-                )
-            for o in range(1, nj):
-                j = lax.rem(me_j + o, nj)
-                send(val_sq.at[me_j], val_sq.at[me_j], v_send.at[j], v_recv.at[me_j], ex * nj + j)
-        if g == 2:
-            ld_ds.wait()
-            down_b[...] = down_sv[...].astype(F32).astype(BF16)
-    ld_us.wait()
-    up_b[...] = up_sv[...].astype(F32).astype(BF16)
+
+    def validation():
+        ld_v.wait()
+        r, c = iota((256, 256), 0), iota((256, 256), 1)
+        per = 256 // cols
+        perm = jnp.where(lax.rem(r, per) * cols + r // per == c, 1.0, 0.0).astype(BF16)
+        ones = jnp.ones((8, own_k), F32)
+        for i in range(nval // per):
+            piece = jnp.dot(perm, val_v[i * 256:(i + 1) * 256, :], preferred_element_type=F32)
+            sq = jnp.zeros((per, own_k), F32)
+            for k in range(cols):
+                rows = piece[k * per:(k + 1) * per]
+                val_p[k, i * per:(i + 1) * per, :] = rows.astype(BF16)
+                sq = sq + rows * rows
+            val_sq[me_j, :, i * per:(i + 1) * per] = lax.dot_general(
+                ones, sq, NT, preferred_element_type=F32, precision=lax.Precision.HIGHEST
+            )
+        for o in range(1, nj):
+            j = lax.rem(me_j + o, nj)
+            send(val_sq.at[me_j], val_sq.at[me_j], v_send.at[j], v_recv.at[me_j], ex * nj + j)
 
     lane = iota((cols, 128), 1)
     row_ex = iota((sub_rows, SUB), 0) // cols
@@ -207,13 +203,23 @@
             jnp.sum(sq, axis=1, keepdims=True), (half_ex, 128)
         )
 
-    mixed(0)
-    mixed(1)
+    per_half = GROUPS // HALVES
+    for g in range(per_half):
+        rank_space(g)
+    ld_ds.wait()
+    down_b[...] = down_sv[...].astype(F32).astype(BF16)
+    ld_us.wait()
+    up_b[...] = up_sv[...].astype(F32).astype(BF16)
+    for g in range(per_half):
+        mixed(g)
     project(0)
-    mixed(2)
+    for g in range(per_half, GROUPS):
+        rank_space(g)
     combine(0)
-    mixed(3)
+    for g in range(per_half, GROUPS):
+        mixed(g)
     project(1)
+    validation()
     combine(1)
     for o in range(1, nj):
         j = lax.rem(me_j + o, nj)
@@ -267,14 +273,6 @@
         for j in range(1, nj):
             acc = acc + dots_r[e, j].astype(F32)
         sim_out[:, e * nval:(e + 1) * nval] = acc * feat_scale
-    ids = tasks[...]
-    onehot = jnp.where(iota((TASKS, ids.shape[1]), 0) == ids, 1.0, 0.0)
-    count = jnp.sum(onehot, axis=1, keepdims=True)
-    score = lax.dot_general(
-        onehot, sim_out[...], NT, preferred_element_type=F32, precision=lax.Precision.HIGHEST
-    ) / jnp.sqrt(count)
-    task_out[...] = score
-    best_out[...] = jnp.max(score, axis=0, keepdims=True)
 
     for o in range(1, nb):
         b = lax.rem(blk + o, nb)
@@ -298,6 +296,19 @@
         return carry
 
     lax.fori_loop(1, n, gone, 0)
+
+
+def finish(sim, tasks, sim_out, task_out, best_out):
+    ids = tasks[...]
+    x = sim[...]
+    onehot = jnp.where(iota((TASKS, ids.shape[1]), 0) == ids, 1.0, 0.0)
+    count = jnp.sum(onehot, axis=1, keepdims=True)
+    score = lax.dot_general(
+        onehot, x, NT, preferred_element_type=F32, precision=lax.Precision.HIGHEST
+    ) / jnp.sqrt(count)
+    sim_out[...] = x
+    task_out[...] = score
+    best_out[...] = jnp.max(score, axis=0, keepdims=True)
 
 
 def body(
@@ -317,15 +328,11 @@
     dma = pltpu.SemaphoreType.DMA
     anyspace = pl.BlockSpec(memory_space=pl.ANY)
     vmem = pl.BlockSpec(memory_space=pltpu.VMEM)
-    sim, score, best = pl.pallas_call(
+    raw = pl.pallas_call(
         functools.partial(kernel, ne, nb, nr, seq, float(krow * cols * nr)),
-        out_shape=(
-            jax.ShapeDtypeStruct((examples, all_val), F32),
-            jax.ShapeDtypeStruct((TASKS, examples), F32),
-            jax.ShapeDtypeStruct((1, examples), F32),
-        ),
-        in_specs=[anyspace] * 7 + [pl.BlockSpec(memory_space=pltpu.SMEM), vmem, vmem],
-        out_specs=(vmem, vmem, vmem),
+        out_shape=jax.ShapeDtypeStruct((examples, all_val), F32),
+        in_specs=[anyspace] * 7 + [pl.BlockSpec(memory_space=pltpu.SMEM), vmem],
+        out_specs=vmem,
         scratch_shapes=[
             pltpu.VMEM((tokens, width), BF16),
             pltpu.VMEM((tokens, width), BF16),
@@ -376,8 +383,17 @@
         jnp.transpose(val, (0, 2, 1)).reshape(nval * cols, own_k),
         lengths,
         jnp.transpose(mixer),
-        tasks.reshape(1, all_val),
     )
+    sim, score, best = pl.pallas_call(
+        finish,
+        out_shape=(
+            jax.ShapeDtypeStruct((examples, all_val), F32),
+            jax.ShapeDtypeStruct((TASKS, examples), F32),
+            jax.ShapeDtypeStruct((1, examples), F32),
+        ),
+        in_specs=[vmem, vmem],
+        out_specs=(vmem, vmem, vmem),
+    )(raw, tasks.reshape(1, all_val))
     return sim, jnp.transpose(score), best.reshape(examples)
 
 

time: 44.8 us -> 40.7 us (0.908)
  local copies, waits for them, and re-layouts: 3.85 us -> 0 us
    unnamed x3 -> x0, local copies, waits for them, and re-layouts: 3.85 us -> none
    pallas_call x1, Pallas kernels: 40.1 us -> 38.3 us  [body(): pl.pallas_call(functools.partial(kernel, ne, nb, nr, seq, float(krow * co...]
    pallas_call x0 -> x1, Pallas kernels: none -> 1.61 us  [body(): pl.pallas_call(finish, out_shape=(jax.ShapeDtypeStruct((examples, all_val...]
where the time goes in v2:
time: 40.7 us; the launch traced here: 40.5 us
  Pallas kernels  39.9 us (98%)
  between operations  0.64 us (2%)
    pallas_call x1, Pallas kernels, body(): pl.pallas_call(functools.partial(kernel, ne, nb, nr, seq, float(krow * co...  38.3 us
    pallas_call x1, Pallas kernels, body(): pl.pallas_call(finish, out_shape=(jax.ShapeDtypeStruct((examples, all_val...  1.61 us

profile of v2, /device:TPU:0, one launch (start us, length us, event | category | flops | bytes accessed | tf_op | source)
XLA Modules:
  0.0 40.5 jit_solution(15323311936063277307)
XLA Ops:
  0.6 38.3 %shard_map.121.sim = f32[32,512]{1,0:T(8,128)} custom-call(bf16[2048,2048]{1,0:T(8,128)(2,1)} %bitcast.9, bf16[2048,2048]{1,0:T(8,128)(2,1)} %bitcast.10, bf16[2048,128]{1,0:T(8,128)(2,1)} %down_w.1, bf16[128,2048]{1,0:T(8,128)(2,1)} %up_w.1, s32[2048,512]{1,0:T(8,128)} %down_s.1, s32[2048,512]{1,0:T(8,128)} %up_s.1, bf16[1024,256]{1,0:T(8,128)(2,1)} %bitcast.11, ...), custom_call_target="tpu_custom_call" | custom-call | tf_op jit(solution)/shard_map/pallas_call | solution.py:331
  38.9 1.6 %shard_map.122 = (f32[32,512]{1,0:T(8,128)}, f32[8,32]{1,0:T(8,128)}, f32[1,32]{1,0:T(1,128)}) custom-call(f32[32,512]{1,0:T(8,128)} %shard_map.121.sim, s32[1,512]{1,0:T(1,128)} %bitcast.13), custom_call_target="tpu_custom_call" | custom-call | tf_op jit(solution)/shard_map/pallas_call | solution.py:387
